TPU v7x, 256 devices: a whole 4x4x8 slice. The times are simulated.
256 devices in a mesh: fsdp: 16 (over x, z_hi, core), frame: 16 (over z_lo, y).
Axes of the slice: x: 4, y: 4, z: 8 (z_hi: 2, z_lo: 4; z = z_hi * 4 + z_lo), core: 2. Of those that a mesh axis runs over, the one named last changes fastest.
Arguments:
- queries: bfloat16 [32, 16, 128, 1536], P('fsdp', 'frame'), may hold values from -6 to 6
- key_vectors: bfloat16 [32, 16, 128, 1536], P('fsdp', 'frame'), may hold values from -6 to 6
- value_vectors: bfloat16 [32, 16, 128, 1536], P('fsdp', 'frame'), may hold values from -6 to 6
- out_weight: bfloat16 [1536, 1536], P(('fsdp', 'frame')), may hold values from -0.15625 to 0.15625
- grad_out: bfloat16 [32, 16, 128, 1536], P('fsdp', 'frame'), may hold values from -6 to 6
Outputs:
- projected: bfloat16 [32, 16, 128, 1536], P('fsdp', 'frame')
- grad_queries: bfloat16 [32, 16, 128, 1536], P('fsdp', 'frame')
- grad_keys: bfloat16 [32, 16, 128, 1536], P('fsdp', 'frame')
- grad_values: bfloat16 [32, 16, 128, 1536], P('fsdp', 'frame')
- grad_weight: float32 [1536, 1536], P(('fsdp', 'frame'))
All inputs are finite; a program needn't handle non-finite values.
Results may differ from a plain program's by a relative error of at most 0.0058.
Values may be sent and summed in bfloat16 or wider, within the bound.
A program may use at most 128 MiB of HBM per device.

v0:
```python
import jax
import jax.numpy as jnp
from jax import lax
from jax.sharding import PartitionSpec as P

HEAD_SIZE = 128


def split_heads(block):
    return block.reshape(block.shape[:-1] + (block.shape[-1] // HEAD_SIZE, HEAD_SIZE))


def pencil_probs(pencil_query, pencil_key):
    scores = jnp.einsum(
        "cfphs,cgphs->cphfg",
        split_heads(pencil_query),
        split_heads(pencil_key),
        preferred_element_type=jnp.float32,
    ) * HEAD_SIZE ** (-0.5)
    index = jnp.arange(pencil_query.shape[1])
    allowed = index[:, None] >= index[None, :]
    scores = jnp.where(allowed, scores, -jnp.inf)
    return jax.nn.softmax(scores, axis=-1)


def local(queries, key_vectors, value_vectors, out_weight, grad_out):
    width = queries.shape[-1]
    out_width = grad_out.shape[-1]
    pencil_query, pencil_key, pencil_value = (
        lax.all_to_all(queries, "frame", split_axis=2, concat_axis=1, tiled=True),
        lax.all_to_all(key_vectors, "frame", split_axis=2, concat_axis=1, tiled=True),
        lax.all_to_all(value_vectors, "frame", split_axis=2, concat_axis=1, tiled=True),
    )
    pencil_shape = pencil_query.shape
    probs = pencil_probs(pencil_query, pencil_key)
    weights = probs.astype(jnp.bfloat16)
    attended = jnp.einsum(
        "cphfg,cgphs->cfphs", weights, split_heads(pencil_value), preferred_element_type=jnp.float32
    )
    attended = attended.astype(jnp.bfloat16).reshape(pencil_shape)
    home = lax.all_to_all(attended, "frame", split_axis=1, concat_axis=2, tiled=True)
    flat = home.reshape(-1, width)
    grad_flat = grad_out.reshape(-1, out_width)
    row_count = flat.shape[0]
    block = lax.all_gather(out_weight, "frame", axis=0, tiled=True)
    total = jnp.dot(
        flat, lax.all_gather(block, "fsdp", axis=0, tiled=True), preferred_element_type=jnp.float32
    )
    grad_attended = lax.dot_general(
        grad_flat,
        lax.all_gather(block, "fsdp", axis=0, tiled=True),
        (((1,), (1,)), ((), ())),
        preferred_element_type=jnp.float32,
    )
    projected_rows = total.astype(jnp.bfloat16)
    grad_rows = grad_attended.astype(jnp.bfloat16)
    projected = projected_rows.reshape(grad_out.shape)
    grad_pencil = lax.all_to_all(
        grad_rows.reshape(queries.shape), "frame", split_axis=2, concat_axis=1, tiled=True
    )
    grad_heads = split_heads(grad_pencil)
    grad_probs = jnp.einsum(
        "cfphs,cgphs->cphfg",
        grad_heads,
        split_heads(pencil_value),
        preferred_element_type=jnp.float32,
    )
    centre = jnp.sum(probs * grad_probs, axis=-1, keepdims=True)
    grad_scores = (probs * (grad_probs - centre)).astype(jnp.bfloat16)
    factor = HEAD_SIZE ** (-0.5)
    grad_query = (
        jnp.einsum(
            "cphfg,cgphs->cfphs",
            grad_scores,
            split_heads(pencil_key),
            preferred_element_type=jnp.float32,
        )
        * factor
    )
    grad_key = (
        jnp.einsum(
            "cphfg,cfphs->cgphs",
            grad_scores,
            split_heads(pencil_query),
            preferred_element_type=jnp.float32,
        )
        * factor
    )
    grad_value = jnp.einsum(
        "cphfg,cfphs->cgphs", weights, grad_heads, preferred_element_type=jnp.float32
    )
    grad_query = grad_query.astype(jnp.bfloat16).reshape(pencil_shape)
    grad_key = grad_key.astype(jnp.bfloat16).reshape(pencil_shape)
    grad_value = grad_value.astype(jnp.bfloat16).reshape(pencil_shape)
    grad_queries, grad_keys, grad_values = (
        lax.all_to_all(grad_query, "frame", split_axis=1, concat_axis=2, tiled=True),
        lax.all_to_all(grad_key, "frame", split_axis=1, concat_axis=2, tiled=True),
        lax.all_to_all(grad_value, "frame", split_axis=1, concat_axis=2, tiled=True),
    )
    fsdp_count = lax.axis_size("fsdp")
    device_count = fsdp_count * lax.axis_size("frame")
    token_factor = float(row_count * device_count) ** (-0.5)
    term = (
        lax.dot_general(
            flat, grad_flat, (((0,), (0,)), ((), ())), preferred_element_type=jnp.float32
        )
        * token_factor
    )
    grad_weight = lax.psum_scatter(term, ("fsdp", "frame"), scatter_dimension=0, tiled=True)
    return (projected, grad_queries, grad_keys, grad_values, grad_weight)


def solution(mesh):
    in_specs = (
        P("fsdp", "frame", None, None),
        P("fsdp", "frame", None, None),
        P("fsdp", "frame", None, None),
        P(("fsdp", "frame"), None),
        P("fsdp", "frame", None, None),
    )
    out_specs = (
        P("fsdp", "frame", None, None),
        P("fsdp", "frame", None, None),
        P("fsdp", "frame", None, None),
        P("fsdp", "frame", None, None),
        P(("fsdp", "frame"), None),
    )
    return jax.shard_map(local, mesh=mesh, in_specs=in_specs, out_specs=out_specs, check_vma=False)
```

profile of v0, /device:TPU:2, one launch (start us, length us, event | category | flops | bytes accessed | tf_op | source)
XLA Modules:
  0.0 1580.3 jit_solution(18264399425220974830)
XLA Ops:
  7.2 46.2 %all-gather = bf16[16,6,1536]{2,1,0:T(8,128)(2,1)S(1)} all-gather(bf16[1,6,1536]{2,1,0:T(8,128)(2,1)} %bitcast.82), channel_id=1, replica_groups=mesh['fsdp'=16,'frame'=16] {'frame'}, dimensions={0}, use_global_device_ids=true | all-gather | bytes 313344 | tf_op jit(solution)/shard_map/all_gather | solution.py:45
  61.4 20.0 %all-to-all-done.2 = bf16[2,1,128,1536]{3,0,1,2:T(2,128)(2,1)S(1)} async-done(((bf16[2,1,128,1536]{3,0,1,2:T(2,128)(2,1)}), bf16[2,1,128,1536]{3,0,1,2:T(2,128)(2,1)S(1)}, u32[]{:S(2)}, u32[]{:S(2)}) %all-to-all-start.2) | async-done | bytes 786464 | tf_op jit(solution)/shard_map/all_to_all | solution.py:32
  81.3 9.8 all-to-all-start.1
  92.8 43.4 %all-to-all-done.1 = bf16[2,1,128,1536]{3,0,1,2:T(2,128)(2,1)S(1)} async-done(((bf16[2,1,128,1536]{3,0,1,2:T(2,128)(2,1)}), bf16[2,1,128,1536]{3,0,1,2:T(2,128)(2,1)S(1)}, u32[]{:S(2)}, u32[]{:S(2)}) %all-to-all-start.1) | async-done | bytes 786464 | tf_op jit(solution)/shard_map/all_to_all | solution.py:31
  136.2 6.6 all-to-all-start
  150.5 6.6 all-to-all-done
  171.5 6.5 all-to-all-done.4
  189.9 11.4 all-to-all-done.3
  209.2 16.8 %all-to-all-done.5 = bf16[2,16,8,1536]{3,2,0,1:T(8,128)(2,1)S(1)} async-done(((bf16[2,16,8,1536]{3,2,0,1:T(8,128)(2,1)}), bf16[2,16,8,1536]{3,2,0,1:T(8,128)(2,1)S(1)}, u32[]{:S(2)}, u32[]{:S(2)}) %all-to-all-start.5) | async-done | bytes 786464 | tf_op jit(solution)/shard_map/all_to_all | solution.py:96
  232.1 5.1 convolution_multiply_fusion
  239.3 10.4 all-to-all-done.6
  249.8 5.2 all-to-all-start.7
  255.0 641.3 %fusion = f32[8,1536]{1,0:T(8,128)S(1)} fusion(f32[1536,1536]{1,0:T(8,128)} %convolution_multiply_fusion), kind=kCustom, calls=%all-reduce-scatter | all-reduce-scatter fusion | flops 3145729 | bytes 9486336
  902.8 67.4 %collective-permute-start.60 = (f32[8,1536]{1,0:T(8,128)S(1)}, f32[8,1536]{1,0:T(8,128)S(1)}, u32[]{:S(2)}, u32[]{:S(2)}) collective-permute-start(f32[8,1536]{1,0:T(8,128)S(1)} %fusion), channel_id=1, source_target_pairs={{0,61},{1,62},{2,63},{3,64},{4,65},{5,66},{6,67},{7,68},{8,69},{9,... | collective-permute-start | bytes 147464
  970.2 8.5 collective-permute-start.63
  1012.3 9.7 collective-permute-start.45
  1062.5 13.7 collective-permute-start.29
  1076.2 13.1 collective-permute-start.28
  1089.3 13.1 collective-permute-start.27
  1102.5 13.1 collective-permute-start.26
  1115.6 13.1 collective-permute-start.25
  1128.8 13.1 collective-permute-start.24
  1141.9 13.1 collective-permute-start.23
  1155.1 13.1 collective-permute-start.22
  1168.2 13.1 collective-permute-start.21
  1181.4 13.1 collective-permute-start.20
  1194.5 13.1 collective-permute-start.19
  1207.7 13.1 collective-permute-start.18
  1220.8 13.1 collective-permute-start.17
  1234.0 13.1 collective-permute-start.16
  1247.1 13.1 collective-permute-start.15
  1260.3 13.1 collective-permute-start.14
  1273.4 13.1 collective-permute-start.13
  1286.6 13.1 collective-permute-start.12
  1299.7 13.1 collective-permute-start.11
  1312.9 13.1 collective-permute-start.10
  1326.0 13.1 collective-permute-start.9
  1339.1 13.1 collective-permute-start.8
  1352.3 13.1 collective-permute-start.7
  1365.4 13.1 collective-permute-start.6
  1378.6 13.1 collective-permute-start.5
  1391.7 13.1 collective-permute-start.4
  1404.8 13.1 collective-permute-start.3
  1418.0 13.1 collective-permute-start.2
  1431.1 13.1 collective-permute-start.1
  1444.3 13.3 collective-permute-start
  1458.1 8.1 collective-permute-done
  1466.2 97.2 %concatenate = f32[518,1536]{1,0:T(8,128)} concatenate(f32[6,1536]{1,0:T(8,128)S(1)} %collective-permute-done.63, f32[8,1536]{1,0:T(8,128)S(1)} %collective-permute-done.62, f32[8,1536]{1,0:T(8,128)S(1)} %collective-permute-done.61, f32[8,1536]{1,0:T(8,128)S(1)} %collective-permute-done.60, f32[8,1536]{1,0:T(8,128)S(1)} %collective-permute-done.59, ...), dimensions={0} | concatenate | bytes 6365184
  (244 shorter events, 149.9 us)
Async XLA Ops:
  7.2 137.9 %all-gather.3.cloned.1.call-start = ((), (), s32[]{:S(2)}) async-start(), calls=%async_computation.8 | async-start | bytes 5013504 | tf_op jit(solution)/shard_map/all_gather | solution.py:47
  56.0 25.3 %all-to-all-start.2 = ((bf16[2,1,128,1536]{3,0,1,2:T(2,128)(2,1)}), bf16[2,1,128,1536]{3,0,1,2:T(2,128)(2,1)S(1)}, u32[]{:S(2)}, u32[]{:S(2)}) async-start(bf16[2,1,128,1536]{3,0,1,2:T(2,128)(2,1)} %copy.67), calls=%async_computation.2 | async-start | bytes 1572864 | tf_op jit(solution)/shard_map/all_to_all | solution.py:32
  81.3 54.8 %all-to-all-start.1 = ((bf16[2,1,128,1536]{3,0,1,2:T(2,128)(2,1)}), bf16[2,1,128,1536]{3,0,1,2:T(2,128)(2,1)S(1)}, u32[]{:S(2)}, u32[]{:S(2)}) async-start(bf16[2,1,128,1536]{3,0,1,2:T(2,128)(2,1)} %copy.63), calls=%async_computation.1 | async-start | bytes 1572864 | tf_op jit(solution)/shard_map/all_to_all | solution.py:31
  136.2 21.0 %all-to-all-start = ((bf16[2,1,128,1536]{3,0,1,2:T(2,128)(2,1)}), bf16[2,1,128,1536]{3,0,1,2:T(2,128)(2,1)S(1)}, u32[]{:S(2)}, u32[]{:S(2)}) async-start(bf16[2,1,128,1536]{3,0,1,2:T(2,128)(2,1)} %copy.61), calls=%async_computation | async-start | bytes 1572864 | tf_op jit(solution)/shard_map/all_to_all | solution.py:30
  158.0 20.0 %all-to-all-start.4 = ((bf16[2,1,128,1536]{3,0,1,2:T(2,128)(2,1)}), bf16[2,1,128,1536]{3,0,1,2:T(2,128)(2,1)S(1)}, u32[]{:S(2)}, u32[]{:S(2)}) async-start(bf16[2,1,128,1536]{3,0,1,2:T(2,128)(2,1)} %copy.74), calls=%async_computation.4 | async-start | bytes 1572864 | tf_op jit(solution)/shard_map/all_to_all | solution.py:58
  178.0 23.3 %all-to-all-start.3 = ((bf16[2,16,8,1536]{3,2,0,1:T(8,128)(2,1)}), bf16[2,16,8,1536]{3,2,0,1:T(8,128)(2,1)S(1)}, u32[]{:S(2)}, u32[]{:S(2)}) async-start(bf16[2,16,8,1536]{3,2,0,1:T(8,128)(2,1)} %copy.72), calls=%async_computation.3 | async-start | bytes 1572864 | tf_op jit(solution)/shard_map/all_to_all | solution.py:41
  202.1 23.8 %all-to-all-start.5 = ((bf16[2,16,8,1536]{3,2,0,1:T(8,128)(2,1)}), bf16[2,16,8,1536]{3,2,0,1:T(8,128)(2,1)S(1)}, u32[]{:S(2)}, u32[]{:S(2)}) async-start(bf16[2,16,8,1536]{3,2,0,1:T(8,128)(2,1)} %copy.81), calls=%async_computation.5 | async-start | bytes 1572864 | tf_op jit(solution)/shard_map/all_to_all | solution.py:96
  226.0 23.8 %all-to-all-start.6 = ((bf16[2,16,8,1536]{3,2,0,1:T(8,128)(2,1)}), bf16[2,16,8,1536]{3,2,0,1:T(8,128)(2,1)S(1)}, u32[]{:S(2)}, u32[]{:S(2)}) async-start(bf16[2,16,8,1536]{3,2,0,1:T(8,128)(2,1)} %copy.85), calls=%async_computation.6 | async-start | bytes 1572864 | tf_op jit(solution)/shard_map/all_to_all | solution.py:97
  249.8 1321.6 %all-to-all-start.7 = ((bf16[2,16,8,1536]{3,2,0,1:T(8,128)(2,1)}), bf16[2,16,8,1536]{3,2,0,1:T(8,128)(2,1)}, u32[]{:S(2)}, u32[]{:S(2)}) async-start(bf16[2,16,8,1536]{3,2,0,1:T(8,128)(2,1)} %copy.89), calls=%async_computation.7 | async-start | bytes 1572864 | tf_op jit(solution)/shard_map/all_to_all | solution.py:98
  896.3 89.1 %collective-permute-start.62 = (f32[8,1536]{1,0:T(8,128)S(1)}, f32[8,1536]{1,0:T(8,128)S(1)}, u32[]{:S(2)}, u32[]{:S(2)}) collective-permute-start(f32[8,1536]{1,0:T(8,128)S(1)} %fusion), channel_id=1, source_target_pairs={{0,63},{1,64},{2,65},{3,66},{4,67},{5,68},{6,69},{7,70},{8,71},{9,... | collective-permute-start | bytes 147464
  900.9 86.4 %collective-permute-start.61 = (f32[8,1536]{1,0:T(8,128)S(1)}, f32[8,1536]{1,0:T(8,128)S(1)}, u32[]{:S(2)}, u32[]{:S(2)}) collective-permute-start(f32[8,1536]{1,0:T(8,128)S(1)} %fusion), channel_id=1, source_target_pairs={{0,62},{1,63},{2,64},{3,65},{4,66},{5,67},{6,68},{7,69},{8,70},{9,... | collective-permute-start | bytes 147464
  902.8 86.4 %collective-permute-start.60 = (f32[8,1536]{1,0:T(8,128)S(1)}, f32[8,1536]{1,0:T(8,128)S(1)}, u32[]{:S(2)}, u32[]{:S(2)}) collective-permute-start(f32[8,1536]{1,0:T(8,128)S(1)} %fusion), channel_id=1, source_target_pairs={{0,61},{1,62},{2,63},{3,64},{4,65},{5,66},{6,67},{7,68},{8,69},{9,... | collective-permute-start | bytes 147464
  1010.4 20.2 %collective-permute-start.46 = (f32[8,1536]{1,0:T(8,128)S(1)}, f32[8,1536]{1,0:T(8,128)S(1)}, u32[]{:S(2)}, u32[]{:S(2)}) collective-permute-start(f32[8,1536]{1,0:T(8,128)S(1)} %fusion), channel_id=1, source_target_pairs={{0,47},{1,48},{2,49},{3,50},{4,51},{5,52},{6,53},{7,54},{8,55},{9,... | collective-permute-start | bytes 147464
  1012.3 20.3 %collective-permute-start.45 = (f32[8,1536]{1,0:T(8,128)S(1)}, f32[8,1536]{1,0:T(8,128)S(1)}, u32[]{:S(2)}, u32[]{:S(2)}) collective-permute-start(f32[8,1536]{1,0:T(8,128)S(1)} %fusion), channel_id=1, source_target_pairs={{0,46},{1,47},{2,48},{3,49},{4,50},{5,51},{6,52},{7,53},{8,54},{9,... | collective-permute-start | bytes 147464
  1051.0 25.2 %collective-permute-start.33 = (f32[8,1536]{1,0:T(8,128)S(1)}, f32[8,1536]{1,0:T(8,128)S(1)}, u32[]{:S(2)}, u32[]{:S(2)}) collective-permute-start(f32[8,1536]{1,0:T(8,128)S(1)} %fusion), channel_id=1, source_target_pairs={{0,34},{1,35},{2,36},{3,37},{4,38},{5,39},{6,40},{7,41},{8,42},{9,... | collective-permute-start | bytes 147464
  1054.6 34.7 %collective-permute-start.32 = (f32[8,1536]{1,0:T(8,128)S(1)}, f32[8,1536]{1,0:T(8,128)S(1)}, u32[]{:S(2)}, u32[]{:S(2)}) collective-permute-start(f32[8,1536]{1,0:T(8,128)S(1)} %fusion), channel_id=1, source_target_pairs={{0,33},{1,34},{2,35},{3,36},{4,37},{5,38},{6,39},{7,40},{8,41},{9,... | collective-permute-start | bytes 147464
  1057.8 44.7 %collective-permute-start.31 = (f32[8,1536]{1,0:T(8,128)S(1)}, f32[8,1536]{1,0:T(8,128)S(1)}, u32[]{:S(2)}, u32[]{:S(2)}) collective-permute-start(f32[8,1536]{1,0:T(8,128)S(1)} %fusion), channel_id=1, source_target_pairs={{0,32},{1,33},{2,34},{3,35},{4,36},{5,37},{6,38},{7,39},{8,40},{9,... | collective-permute-start | bytes 147464
  1060.5 55.1 %collective-permute-start.30 = (f32[8,1536]{1,0:T(8,128)S(1)}, f32[8,1536]{1,0:T(8,128)S(1)}, u32[]{:S(2)}, u32[]{:S(2)}) collective-permute-start(f32[8,1536]{1,0:T(8,128)S(1)} %fusion), channel_id=1, source_target_pairs={{0,31},{1,32},{2,33},{3,34},{4,35},{5,36},{6,37},{7,38},{8,39},{9,... | collective-permute-start | bytes 147464
  1062.5 66.3 %collective-permute-start.29 = (f32[8,1536]{1,0:T(8,128)S(1)}, f32[8,1536]{1,0:T(8,128)S(1)}, u32[]{:S(2)}, u32[]{:S(2)}) collective-permute-start(f32[8,1536]{1,0:T(8,128)S(1)} %fusion), channel_id=1, source_target_pairs={{0,30},{1,31},{2,32},{3,33},{4,34},{5,35},{6,36},{7,37},{8,38},{9,... | collective-permute-start | bytes 147464
  1076.2 65.7 %collective-permute-start.28 = (f32[8,1536]{1,0:T(8,128)S(1)}, f32[8,1536]{1,0:T(8,128)S(1)}, u32[]{:S(2)}, u32[]{:S(2)}) collective-permute-start(f32[8,1536]{1,0:T(8,128)S(1)} %fusion), channel_id=1, source_target_pairs={{0,29},{1,30},{2,31},{3,32},{4,33},{5,34},{6,35},{7,36},{8,37},{9,... | collective-permute-start | bytes 147464
  1089.3 65.7 %collective-permute-start.27 = (f32[8,1536]{1,0:T(8,128)S(1)}, f32[8,1536]{1,0:T(8,128)S(1)}, u32[]{:S(2)}, u32[]{:S(2)}) collective-permute-start(f32[8,1536]{1,0:T(8,128)S(1)} %fusion), channel_id=1, source_target_pairs={{0,28},{1,29},{2,30},{3,31},{4,32},{5,33},{6,34},{7,35},{8,36},{9,... | collective-permute-start | bytes 147464
  1102.5 65.7 %collective-permute-start.26 = (f32[8,1536]{1,0:T(8,128)S(1)}, f32[8,1536]{1,0:T(8,128)S(1)}, u32[]{:S(2)}, u32[]{:S(2)}) collective-permute-start(f32[8,1536]{1,0:T(8,128)S(1)} %fusion), channel_id=1, source_target_pairs={{0,27},{1,28},{2,29},{3,30},{4,31},{5,32},{6,33},{7,34},{8,35},{9,... | collective-permute-start | bytes 147464
  1115.6 65.7 %collective-permute-start.25 = (f32[8,1536]{1,0:T(8,128)S(1)}, f32[8,1536]{1,0:T(8,128)S(1)}, u32[]{:S(2)}, u32[]{:S(2)}) collective-permute-start(f32[8,1536]{1,0:T(8,128)S(1)} %fusion), channel_id=1, source_target_pairs={{0,26},{1,27},{2,28},{3,29},{4,30},{5,31},{6,32},{7,33},{8,34},{9,... | collective-permute-start | bytes 147464
  1128.8 65.7 %collective-permute-start.24 = (f32[8,1536]{1,0:T(8,128)S(1)}, f32[8,1536]{1,0:T(8,128)S(1)}, u32[]{:S(2)}, u32[]{:S(2)}) collective-permute-start(f32[8,1536]{1,0:T(8,128)S(1)} %fusion), channel_id=1, source_target_pairs={{0,25},{1,26},{2,27},{3,28},{4,29},{5,30},{6,31},{7,32},{8,33},{9,... | collective-permute-start | bytes 147464
  1141.9 65.7 %collective-permute-start.23 = (f32[8,1536]{1,0:T(8,128)S(1)}, f32[8,1536]{1,0:T(8,128)S(1)}, u32[]{:S(2)}, u32[]{:S(2)}) collective-permute-start(f32[8,1536]{1,0:T(8,128)S(1)} %fusion), channel_id=1, source_target_pairs={{0,24},{1,25},{2,26},{3,27},{4,28},{5,29},{6,30},{7,31},{8,32},{9,... | collective-permute-start | bytes 147464
  1155.1 65.7 %collective-permute-start.22 = (f32[8,1536]{1,0:T(8,128)S(1)}, f32[8,1536]{1,0:T(8,128)S(1)}, u32[]{:S(2)}, u32[]{:S(2)}) collective-permute-start(f32[8,1536]{1,0:T(8,128)S(1)} %fusion), channel_id=1, source_target_pairs={{0,23},{1,24},{2,25},{3,26},{4,27},{5,28},{6,29},{7,30},{8,31},{9,... | collective-permute-start | bytes 147464
  1168.2 65.7 %collective-permute-start.21 = (f32[8,1536]{1,0:T(8,128)S(1)}, f32[8,1536]{1,0:T(8,128)S(1)}, u32[]{:S(2)}, u32[]{:S(2)}) collective-permute-start(f32[8,1536]{1,0:T(8,128)S(1)} %fusion), channel_id=1, source_target_pairs={{0,22},{1,23},{2,24},{3,25},{4,26},{5,27},{6,28},{7,29},{8,30},{9,... | collective-permute-start | bytes 147464
  1181.4 65.7 %collective-permute-start.20 = (f32[8,1536]{1,0:T(8,128)S(1)}, f32[8,1536]{1,0:T(8,128)S(1)}, u32[]{:S(2)}, u32[]{:S(2)}) collective-permute-start(f32[8,1536]{1,0:T(8,128)S(1)} %fusion), channel_id=1, source_target_pairs={{0,21},{1,22},{2,23},{3,24},{4,25},{5,26},{6,27},{7,28},{8,29},{9,... | collective-permute-start | bytes 147464
  1194.5 65.7 %collective-permute-start.19 = (f32[8,1536]{1,0:T(8,128)S(1)}, f32[8,1536]{1,0:T(8,128)S(1)}, u32[]{:S(2)}, u32[]{:S(2)}) collective-permute-start(f32[8,1536]{1,0:T(8,128)S(1)} %fusion), channel_id=1, source_target_pairs={{0,20},{1,21},{2,22},{3,23},{4,24},{5,25},{6,26},{7,27},{8,28},{9,... | collective-permute-start | bytes 147464
  1207.7 65.7 %collective-permute-start.18 = (f32[8,1536]{1,0:T(8,128)S(1)}, f32[8,1536]{1,0:T(8,128)S(1)}, u32[]{:S(2)}, u32[]{:S(2)}) collective-permute-start(f32[8,1536]{1,0:T(8,128)S(1)} %fusion), channel_id=1, source_target_pairs={{0,19},{1,20},{2,21},{3,22},{4,23},{5,24},{6,25},{7,26},{8,27},{9,... | collective-permute-start | bytes 147464
  1220.8 65.7 %collective-permute-start.17 = (f32[8,1536]{1,0:T(8,128)S(1)}, f32[8,1536]{1,0:T(8,128)}, u32[]{:S(2)}, u32[]{:S(2)}) collective-permute-start(f32[8,1536]{1,0:T(8,128)S(1)} %fusion), channel_id=1, source_target_pairs={{0,18},{1,19},{2,20},{3,21},{4,22},{5,23},{6,24},{7,25},{8,26},{9,... | collective-permute-start | bytes 147464
  1234.0 65.7 %collective-permute-start.16 = (f32[8,1536]{1,0:T(8,128)S(1)}, f32[8,1536]{1,0:T(8,128)}, u32[]{:S(2)}, u32[]{:S(2)}) collective-permute-start(f32[8,1536]{1,0:T(8,128)S(1)} %fusion), channel_id=1, source_target_pairs={{0,17},{1,18},{2,19},{3,20},{4,21},{5,22},{6,23},{7,24},{8,25},{9,... | collective-permute-start | bytes 147464
  1247.1 65.7 %collective-permute-start.15 = (f32[8,1536]{1,0:T(8,128)S(1)}, f32[8,1536]{1,0:T(8,128)}, u32[]{:S(2)}, u32[]{:S(2)}) collective-permute-start(f32[8,1536]{1,0:T(8,128)S(1)} %fusion), channel_id=1, source_target_pairs={{0,16},{1,17},{2,18},{3,19},{4,20},{5,21},{6,22},{7,23},{8,24},{9,... | collective-permute-start | bytes 147464
  1260.3 65.7 %collective-permute-start.14 = (f32[8,1536]{1,0:T(8,128)S(1)}, f32[8,1536]{1,0:T(8,128)}, u32[]{:S(2)}, u32[]{:S(2)}) collective-permute-start(f32[8,1536]{1,0:T(8,128)S(1)} %fusion), channel_id=1, source_target_pairs={{0,15},{1,16},{2,17},{3,18},{4,19},{5,20},{6,21},{7,22},{8,23},{9,... | collective-permute-start | bytes 147464
  1273.4 65.7 %collective-permute-start.13 = (f32[8,1536]{1,0:T(8,128)S(1)}, f32[8,1536]{1,0:T(8,128)}, u32[]{:S(2)}, u32[]{:S(2)}) collective-permute-start(f32[8,1536]{1,0:T(8,128)S(1)} %fusion), channel_id=1, source_target_pairs={{0,14},{1,15},{2,16},{3,17},{4,18},{5,19},{6,20},{7,21},{8,22},{9,... | collective-permute-start | bytes 147464
  1286.6 65.7 %collective-permute-start.12 = (f32[8,1536]{1,0:T(8,128)S(1)}, f32[8,1536]{1,0:T(8,128)}, u32[]{:S(2)}, u32[]{:S(2)}) collective-permute-start(f32[8,1536]{1,0:T(8,128)S(1)} %fusion), channel_id=1, source_target_pairs={{0,13},{1,14},{2,15},{3,16},{4,17},{5,18},{6,19},{7,20},{8,21},{9,... | collective-permute-start | bytes 147464
  1299.7 65.7 %collective-permute-start.11 = (f32[8,1536]{1,0:T(8,128)S(1)}, f32[8,1536]{1,0:T(8,128)}, u32[]{:S(2)}, u32[]{:S(2)}) collective-permute-start(f32[8,1536]{1,0:T(8,128)S(1)} %fusion), channel_id=1, source_target_pairs={{0,12},{1,13},{2,14},{3,15},{4,16},{5,17},{6,18},{7,19},{8,20},{9,... | collective-permute-start | bytes 147464
  1312.9 65.7 %collective-permute-start.10 = (f32[8,1536]{1,0:T(8,128)S(1)}, f32[8,1536]{1,0:T(8,128)}, u32[]{:S(2)}, u32[]{:S(2)}) collective-permute-start(f32[8,1536]{1,0:T(8,128)S(1)} %fusion), channel_id=1, source_target_pairs={{0,11},{1,12},{2,13},{3,14},{4,15},{5,16},{6,17},{7,18},{8,19},{9,... | collective-permute-start | bytes 147464
  1326.0 65.7 %collective-permute-start.9 = (f32[8,1536]{1,0:T(8,128)S(1)}, f32[8,1536]{1,0:T(8,128)}, u32[]{:S(2)}, u32[]{:S(2)}) collective-permute-start(f32[8,1536]{1,0:T(8,128)S(1)} %fusion), channel_id=1, source_target_pairs={{0,10},{1,11},{2,12},{3,13},{4,14},{5,15},{6,16},{7,17},{8,18},{9,... | collective-permute-start | bytes 147464
  1339.1 65.7 %collective-permute-start.8 = (f32[8,1536]{1,0:T(8,128)S(1)}, f32[8,1536]{1,0:T(8,128)}, u32[]{:S(2)}, u32[]{:S(2)}) collective-permute-start(f32[8,1536]{1,0:T(8,128)S(1)} %fusion), channel_id=1, source_target_pairs={{0,9},{1,10},{2,11},{3,12},{4,13},{5,14},{6,15},{7,16},{8,17},{9,1... | collective-permute-start | bytes 147464
  1352.3 65.7 %collective-permute-start.7 = (f32[8,1536]{1,0:T(8,128)S(1)}, f32[8,1536]{1,0:T(8,128)}, u32[]{:S(2)}, u32[]{:S(2)}) collective-permute-start(f32[8,1536]{1,0:T(8,128)S(1)} %fusion), channel_id=1, source_target_pairs={{0,8},{1,9},{2,10},{3,11},{4,12},{5,13},{6,14},{7,15},{8,16},{9,17... | collective-permute-start | bytes 147464
  1365.4 65.7 %collective-permute-start.6 = (f32[8,1536]{1,0:T(8,128)S(1)}, f32[8,1536]{1,0:T(8,128)}, u32[]{:S(2)}, u32[]{:S(2)}) collective-permute-start(f32[8,1536]{1,0:T(8,128)S(1)} %fusion), channel_id=1, source_target_pairs={{0,7},{1,8},{2,9},{3,10},{4,11},{5,12},{6,13},{7,14},{8,15},{9,16}... | collective-permute-start | bytes 147464
  1378.6 65.7 %collective-permute-start.5 = (f32[8,1536]{1,0:T(8,128)S(1)}, f32[8,1536]{1,0:T(8,128)}, u32[]{:S(2)}, u32[]{:S(2)}) collective-permute-start(f32[8,1536]{1,0:T(8,128)S(1)} %fusion), channel_id=1, source_target_pairs={{0,6},{1,7},{2,8},{3,9},{4,10},{5,11},{6,12},{7,13},{8,14},{9,15},... | collective-permute-start | bytes 147464
  1391.7 66.3 %collective-permute-start.4 = (f32[8,1536]{1,0:T(8,128)S(1)}, f32[8,1536]{1,0:T(8,128)}, u32[]{:S(2)}, u32[]{:S(2)}) collective-permute-start(f32[8,1536]{1,0:T(8,128)S(1)} %fusion), channel_id=1, source_target_pairs={{0,5},{1,6},{2,7},{3,8},{4,9},{5,10},{6,11},{7,12},{8,13},{9,14},{... | collective-permute-start | bytes 147464
  1404.8 53.2 %collective-permute-start.3 = (f32[8,1536]{1,0:T(8,128)S(1)}, f32[8,1536]{1,0:T(8,128)}, u32[]{:S(2)}, u32[]{:S(2)}) collective-permute-start(f32[8,1536]{1,0:T(8,128)S(1)} %fusion), channel_id=1, source_target_pairs={{0,4},{1,5},{2,6},{3,7},{4,8},{5,9},{6,10},{7,11},{8,12},{9,13},{1... | collective-permute-start | bytes 147464
  1418.0 40.1 %collective-permute-start.2 = (f32[8,1536]{1,0:T(8,128)S(1)}, f32[8,1536]{1,0:T(8,128)}, u32[]{:S(2)}, u32[]{:S(2)}) collective-permute-start(f32[8,1536]{1,0:T(8,128)S(1)} %fusion), channel_id=1, source_target_pairs={{0,3},{1,4},{2,5},{3,6},{4,7},{5,8},{6,9},{7,10},{8,11},{9,12},{10... | collective-permute-start | bytes 147464
  1431.1 26.9 %collective-permute-start.1 = (f32[8,1536]{1,0:T(8,128)S(1)}, f32[8,1536]{1,0:T(8,128)}, u32[]{:S(2)}, u32[]{:S(2)}) collective-permute-start(f32[8,1536]{1,0:T(8,128)S(1)} %fusion), channel_id=1, source_target_pairs={{0,2},{1,3},{2,4},{3,5},{4,6},{5,7},{6,8},{7,9},{8,10},{9,11},{10,... | collective-permute-start | bytes 147464
  1444.3 21.9 %collective-permute-start = (f32[8,1536]{1,0:T(8,128)S(1)}, f32[8,1536]{1,0:T(8,128)}, u32[]{:S(2)}, u32[]{:S(2)}) collective-permute-start(f32[8,1536]{1,0:T(8,128)S(1)} %fusion), channel_id=1, source_target_pairs={{0,1},{1,2},{2,3},{3,4},{4,5},{5,6},{6,7},{7,8},{8,9},{9,10},{10,1... | collective-permute-start | bytes 147464
  (79 other events, 14931.6 us)
Sparse Core Ops, SparseCore 0:
  54.4 90.6 all-gather.2
where the time goes:
time: 1590 us; the launch traced here: 1580 us
  blocking collectives  688 us (43%)
  starting transfers between devices  597 us (38%)
  waiting for transfers between devices  132 us (8%)
  local copies, waits for them, and re-layouts  125 us (8%)
  matrix products  22.1 us (1%)
  between operations  15.9 us (1%)
    unnamed x1, blocking collectives  641 us
    unnamed x64, starting transfers between devices  553 us
    unnamed x115, local copies, waits for them, and re-layouts  110 us
    all_gather x1, blocking collectives, local(): block = lax.all_gather(out_weight, 'frame', axis=0, tiled=True)  46.2 us
    all_to_all x1, waiting for transfers between devices, local(): lax.all_to_all(key_vectors, 'frame', split_axis=2, concat_axis=1, tiled=T...  43.4 us
  transfers between devices with their start and end apart: 73, of which 15 were waited for; matrix products, arithmetic and copies ran while one was open for 49% of the time, Pallas kernels for 0%

commit v1 on v0

v1 whole, which is shorter than its diff:
```python
import functools

import jax
import jax.numpy as jnp
from jax import lax
from jax.experimental import pallas as pl
from jax.experimental.pallas import tpu as pltpu
from jax.sharding import PartitionSpec as P

MESH = pl.DeviceIdType.MESH
F32, BF16 = jnp.float32, jnp.bfloat16
HEAD = 128
ROWS = 256
PART = 64
BAND = 16
WIDTH = 1536
LANES = 512
FACTOR = HEAD ** -0.5
TOKEN_FACTOR = 65536.0 ** -0.5
SETS = ((0, 1, 1, 1), (0, 0, 3, 3), (0, 1, 2, 2))
Q, K, V, G = range(4)
NT = (((1,), (1,)), ((), ()))
TN = (((0,), (0,)), ((), ()))


def dot(a, b, dims=(((1,), (0,)), ((), ()))):
    return lax.dot_general(a, b, dims, preferred_element_type=F32)


def query_blocks(site, where):
    return [b for b in range(4) if where[b] == site]


def key_sites(block, where):
    return [s for s in sorted(set(where)) if block <= max(query_blocks(s, where))]


def lanes_of(s):
    return pl.ds(LANES * s, LANES)


def kernel(q_in, k_in, v_in, w_in, g_in, proj_out, dq_out, dk_out, dv_out, dw_out, *refs):
    refs = list(refs)
    take = lambda n: [refs.pop(0) for _ in range(n)]
    held = [take(4) for _ in SETS]
    attended = take(len(SETS))
    g_home, o_home, ga_home, partial, proj_home = take(5)
    w_slabs, w_pad, w_full = take(3)
    dw_part, core_in, x_out, x_in, y_out, y_in, z_out, z_in = take(8)
    local_sem, in_send, in_recv, o_send, o_recv, back_send, back_recv = take(7)
    wz_send, wz_recv, wy_send, wy_recv, wx_send, wx_recv, wc_send, wc_recv = take(8)
    dc_send, dc_recv, dx_send, dx_recv, dy_send, dy_recv, dz_send, dz_recv = take(8)

    f = lax.axis_index("fsdp")
    fr = lax.axis_index("frame")
    x, zh, core = f // 4, lax.rem(f // 2, 2), lax.rem(f, 2)
    z, y = fr // 4, lax.rem(fr, 4)
    z8 = zh * 4 + z

    def z_device(d):
        t = lax.rem(z8 + d, 8)
        return {"fsdp": x * 4 + (t // 4) * 2 + core, "frame": lax.rem(t, 4) * 4 + y}

    def y_device(d):
        return {"frame": z * 4 + lax.rem(y + d, 4)}

    def x_device(d):
        return {"fsdp": lax.rem(x + d, 4) * 4 + lax.rem(f, 4)}

    other_core = {"fsdp": f + 1 - 2 * core}

    def remote(src, dst, send, recv, device):
        return pltpu.make_async_remote_copy(
            src_ref=src, dst_ref=dst, send_sem=send, recv_sem=recv, device_id=device, device_id_type=MESH
        )

    def wait_slabs(sem, n):
        ref = held[0][0].at[pl.ds(0, n)]
        pltpu.make_async_copy(ref, ref, sem).wait()

    barrier = pltpu.get_barrier_semaphore()
    for d in range(1, 16):
        pl.semaphore_signal(barrier, inc=1, device_id={"frame": lax.rem(fr + d, 16)}, device_id_type=MESH)
    for d in (1, 2, 3):
        pl.semaphore_signal(barrier, inc=1, device_id=x_device(d), device_id_type=MESH)
    pl.semaphore_signal(barrier, inc=1, device_id=other_core, device_id_type=MESH)
    for k in range(4):
        device = {"fsdp": x * 4 + (1 - zh) * 2 + core, "frame": k * 4 + y}
        pl.semaphore_signal(barrier, inc=1, device_id=device, device_id_type=MESH)
    pl.semaphore_wait(barrier, 23)

    g_load = pltpu.make_async_copy(g_in, g_home, local_sem.at[0])
    g_load.start()
    own_rows = pltpu.make_async_copy(w_in, w_slabs.at[y, z8], local_sem.at[1])
    own_rows.start()
    wz = [
        remote(w_in, w_slabs.at[y, z8], wz_send.at[d], wz_recv.at[d], z_device(d)) for d in range(1, 8)
    ]
    for c in wz:
        c.start()

    def for_each_z(fn):
        for zs in range(4):
            pl.when(z == zs)(functools.partial(fn, zs))

    sent = {}

    def send_in(zs, t, s):
        where = SETS[s]
        src = (q_in, k_in, v_in, ga_home)[t]
        sites = [where[zs]] if t in (Q, G) else key_sites(zs, where)
        count = 0
        for site in sorted(sites, key=lambda a: -abs(a - zs)):

            def part(j):
                return src.at[pl.ds(pl.multiple_of(j * PART, PART), PART), lanes_of(s)]

            def send(dy):
                j = lax.rem(y + dy, 4)
                remote(
                    part(j), held[s][t].at[fr], in_send.at[t, s], in_recv.at[t, s], {"frame": site * 4 + j}
                ).start()

            for dy in (1, 2, 3):
                send(dy)
            if site == zs:
                pltpu.make_async_copy(part(y), held[s][t].at[fr], in_recv.at[t, s]).start()
                count += 3
            else:
                send(0)
                count += 4
        sent[zs, t, s] = count

    def wait_in(zs, t, s):
        blocks = query_blocks(zs, SETS[s])
        wait_slabs(in_recv.at[t, s], 4 * len(blocks) if t in (Q, G) else 4 * (max(blocks) + 1))

    def home_rows(ref, s):
        return ref.at[pl.ds(pl.multiple_of(y * PART, PART), PART), lanes_of(s)]

    def send_home(zs, s, src, blocks, dst_of, send_sem, recv_of):
        count = 0
        for b in blocks:
            for k in (1, 2, 3, 0):
                frame = 4 * b + lax.rem(y + k, 4)
                if b == zs and k == 0:
                    pltpu.make_async_copy(src.at[frame], dst_of(b), recv_of(b)).start()
                else:
                    remote(src.at[frame], dst_of(b), send_sem, recv_of(b), {"frame": frame}).start()
                    count += 1
        return count

    def geometry(zs, s):
        blocks = query_blocks(zs, SETS[s])
        return 4 * blocks[0], 4 * (blocks[-1] + 1), 4 * (blocks[-1] + 1)

    def bias_of(first, last, keys):
        shape = ((last - first) * BAND, keys * BAND)
        row = lax.broadcasted_iota(jnp.int32, shape, 0)
        col = lax.broadcasted_iota(jnp.int32, shape, 1)
        allowed = ((row & 15) == (col & 15)) & ((row >> 4) + first >= (col >> 4))
        return jnp.where(allowed, 0.0, -jnp.inf).astype(F32)

    def probs_of(queries, keys, bias):
        scores = dot(queries, keys, NT) * FACTOR + bias
        top = jnp.max(scores, axis=1, keepdims=True)
        e = jnp.exp(scores - top)
        return e / jnp.sum(e, axis=1, keepdims=True)

    def bands(fn):
        def step(h, carry):
            lanes = pl.ds(pl.multiple_of(h * HEAD, HEAD), HEAD)
            for p in range(4):
                fn(pl.ds(p * BAND, BAND), lanes)
            return carry

        lax.fori_loop(0, 4, step, 0)

    def forward(zs, s):
        first, last, keys = geometry(zs, s)
        for t in (Q, K, V):
            wait_in(zs, t, s)
        bias = bias_of(first, last, keys)

        def band(rows, lanes):
            load = lambda t, a, b: held[s][t][a:b, rows, lanes].reshape((b - a) * BAND, HEAD)
            weights = probs_of(load(Q, first, last), load(K, 0, keys), bias).astype(BF16)
            out = dot(weights, load(V, 0, keys)).astype(BF16)
            attended[s][first:last, rows, lanes] = out.reshape(last - first, BAND, HEAD)

        bands(band)
        sent[zs, "o", s] = send_home(
            zs, s, attended[s], query_blocks(zs, SETS[s]), lambda b: home_rows(o_home, s), o_send.at[s],
            lambda b: o_recv.at[s],
        )

    def backward(zs, s):
        first, last, keys = geometry(zs, s)
        wait_in(zs, G, s)
        bias = bias_of(first, last, keys)

        def band(rows, lanes):
            load = lambda t, a, b: held[s][t][a:b, rows, lanes].reshape((b - a) * BAND, HEAD)
            queries, keys_, values, grads = load(Q, first, last), load(K, 0, keys), load(V, 0, keys), load(G, first, last)
            probs = probs_of(queries, keys_, bias)
            grad_probs = dot(grads, values, NT)
            centre = jnp.sum(probs * grad_probs, axis=1, keepdims=True)
            grad_scores = (probs * (grad_probs - centre)).astype(BF16)
            weights = probs.astype(BF16)
            grad_q = (dot(grad_scores, keys_) * FACTOR).astype(BF16)
            grad_k = (dot(grad_scores, queries, TN) * FACTOR).astype(BF16)
            grad_v = dot(weights, grads, TN).astype(BF16)
            held[s][Q][first:last, rows, lanes] = grad_q.reshape(last - first, BAND, HEAD)
            held[s][K][0:keys, rows, lanes] = grad_k.reshape(keys, BAND, HEAD)
            held[s][V][0:keys, rows, lanes] = grad_v.reshape(keys, BAND, HEAD)

        bands(band)
        sent[zs, "q", s] = send_home(
            zs, s, held[s][Q], query_blocks(zs, SETS[s]), lambda b: home_rows(dq_out, s), back_send.at[0, s],
            lambda b: back_recv.at[0, s, 0],
        )
        for t, out in ((K, dk_out), (V, dv_out)):

            def dst_of(b, t=t, out=out):
                sites = key_sites(b, SETS[s])
                ref = out if len(sites) == 1 else partial.at[t - K, sites.index(zs)]
                return home_rows(ref, s)

            sent[zs, ("k", "v")[t - K], s] = send_home(
                zs, s, held[s][t], range(keys // 4), dst_of, back_send.at[t, s],
                lambda b, t=t: back_recv.at[t, s, key_sites(b, SETS[s]).index(zs)],
            )

    def each_set(fn):
        def at(zs):
            for s in range(len(SETS)):
                if zs in SETS[s]:
                    fn(zs, s)

        for_each_z(at)

    def send_qkv(s):
        for_each_z(lambda zs: [send_in(zs, t, s) for t in (Q, K, V)] and None)

    def at_sites(fn, s):
        for zs in sorted(set(SETS[s])):
            pl.when(z == zs)(functools.partial(fn, zs, s))

    send_qkv(0)

    for c in wz:
        c.wait()
    own_rows.wait()
    wy = [
        remote(w_slabs.at[y], w_slabs.at[y], wy_send.at[d], wy_recv.at[d], y_device(d)) for d in (1, 2, 3)
    ]
    for c in wy:
        c.start()

    send_qkv(1)
    send_qkv(2)

    w_pad[...] = jnp.zeros_like(w_pad)
    r = lax.broadcasted_iota(jnp.int32, (96, 128), 0)
    c_ = lax.broadcasted_iota(jnp.int32, (96, 128), 1)
    sixth = (r * 171) >> 10
    pick = jnp.where(c_ == r + 2 * sixth, 1.0, 0.0).astype(BF16)
    for c in wy:
        c.wait()

    def w_rows(xx, h, cc):
        return w_full.at[pl.ds(pl.multiple_of((4 * xx + 2 * h + cc) * 96, 96), 96)]

    def x_from(d):
        return lax.rem(x + 4 - d, 4)

    def core_copy(d, h):
        return remote(w_rows(x_from(d), h, core), w_rows(x_from(d), h, core), wc_send.at[d, h], wc_recv.at[d, h], other_core)

    wx = {}
    for h in range(2):
        for i in range(16):
            w_pad[8 * i : 8 * i + 6, :] = w_slabs[i % 4, 4 * h + i // 4].astype(F32)
        w_rows(x, h, core)[...] = dot(pick, w_pad[...].astype(BF16)).astype(BF16)
        for d in (1, 2, 3):
            wx[d, h] = remote(w_rows(x, h, core), w_rows(x, h, core), wx_send.at[d, h], wx_recv.at[d, h], x_device(d))
            wx[d, h].start()
        core_copy(0, h).start()

    at_sites(forward, 0)

    for d in (1, 2, 3):
        for h in range(2):
            wx[d, h].wait()
            core_copy(d, h).start()

    at_sites(forward, 1)
    at_sites(forward, 2)

    for d in range(4):
        for h in range(2):
            core_copy(d, h).wait()
    g_load.wait()
    for s in range(len(SETS)):
        ga_home[:, lanes_of(s)] = dot(g_home[...], w_full[LANES * s : LANES * (s + 1), :], NT).astype(BF16)
        for_each_z(lambda zs: send_in(zs, G, s))

    for s in range(len(SETS)):
        wait_slabs(o_recv.at[s], 4)

    def dw_rows(xx, h, cc):
        return pl.ds(pl.multiple_of((4 * xx + 2 * h + cc) * 96, 96), 96)

    dc = {}
    for d in (1, 2, 3, 0):
        xx = lax.rem(x + d, 4)
        block = pl.ds(pl.multiple_of(xx * 384, 384), 384)
        left = o_home[:, block]
        for n in range(3):
            cols = pl.ds(n * LANES, LANES)
            dw_part[block, cols] = (dot(left, g_home[:, cols], TN) * TOKEN_FACTOR).astype(BF16)
        for h in range(2):
            dc[d, h] = remote(
                dw_part.at[dw_rows(xx, h, 1 - core)], core_in.at[d, h], dc_send.at[d, h], dc_recv.at[d, h], other_core
            )
            dc[d, h].start()

    at_sites(backward, 0)

    dx = {}
    for d in (1, 2, 3, 0):
        xx = lax.rem(x + d, 4)
        for h in range(2):
            dc[d, h].wait()
            x_out[d, h * 96 : (h + 1) * 96, :] = (
                dw_part[dw_rows(xx, h, core), :].astype(F32) + core_in[d, h].astype(F32)
            ).astype(BF16)
        if d:
            dx[d] = remote(x_out.at[d], x_in.at[d], dx_send.at[d], dx_recv.at[d], x_device(d))
            dx[d].start()

    at_sites(backward, 1)
    at_sites(backward, 2)

    for n in range(3):
        cols = pl.ds(n * LANES, LANES)
        proj_home[:, cols] = dot(o_home[...], w_full[:, cols]).astype(BF16)
    proj_copy = pltpu.make_async_copy(proj_home, proj_out, local_sem.at[2])
    proj_copy.start()

    for d in (1, 2, 3):
        dx[d].wait()
    r = lax.broadcasted_iota(jnp.int32, (192, 192), 0)
    c_ = lax.broadcasted_iota(jnp.int32, (192, 192), 1)
    slab = (r * 171) >> 10
    source = 24 * (slab & 7) + 6 * (slab >> 3) + (r - 6 * slab)
    order = jnp.where(c_ == source, 1.0, 0.0).astype(BF16)
    for n in range(3):
        cols = pl.ds(n * LANES, LANES)
        total = x_out[0, :, cols].astype(F32)
        for d in (1, 2, 3):
            total += x_in[d, :, cols].astype(F32)
        y_out[:, :, cols] = dot(order, total.astype(BF16)).astype(BF16).reshape(4, 48, LANES)
    dy = {}
    for d in (1, 2, 3):
        dy[d] = remote(y_out.at[lax.rem(y + d, 4)], y_in.at[d], dy_send.at[d], dy_recv.at[d], y_device(d))
        dy[d].start()
    for d in (1, 2, 3):
        dy[d].wait()
    r = lax.broadcasted_iota(jnp.int32, (64, 48), 0)
    c_ = lax.broadcasted_iota(jnp.int32, (64, 48), 1)
    spread = jnp.where((c_ == r - 2 * (r >> 3)) & ((r & 7) < 6), 1.0, 0.0).astype(BF16)
    total = y_out[y].astype(F32)
    for d in (1, 2, 3):
        total += y_in[d].astype(F32)
    slabs = dot(spread, total.astype(BF16))
    for i in range(8):
        z_out[i] = slabs[8 * i : 8 * i + 6].astype(BF16)
    dz = {}
    for d in range(1, 8):
        dz[d] = remote(z_out.at[lax.rem(z8 + d, 8)], z_in.at[d], dz_send.at[d], dz_recv.at[d], z_device(d))
        dz[d].start()

    def finish(zs):
        for s in range(len(SETS)):
            n = len(key_sites(zs, SETS[s]))
            for t, out in ((K, dk_out), (V, dv_out)):
                for site in range(n):
                    wait_slabs(back_recv.at[t, s, site], 4)
                if n > 1:
                    terms = partial.at[t - K]

                    def add(i, carry, terms=terms, n=n, s=s):
                        rows = pl.ds(pl.multiple_of(i * PART, PART), PART)
                        total = terms[0, rows, lanes_of(s)].astype(F32)
                        for site in range(1, n):
                            total += terms[site, rows, lanes_of(s)].astype(F32)
                        terms[0, rows, lanes_of(s)] = total.astype(BF16)
                        return carry

                    lax.fori_loop(0, ROWS // PART, add, 0)
                    pltpu.make_async_copy(
                        terms.at[0, :, lanes_of(s)], out.at[:, lanes_of(s)], back_recv.at[t, s, 0]
                    ).start()
            wait_slabs(back_recv.at[0, s, 0], 4)

    for_each_z(finish)

    for d in range(1, 8):
        dz[d].wait()
    total = z_out[z8].astype(F32)
    for d in range(1, 8):
        total += z_in[d].astype(F32)
    dw_out[...] = total

    proj_copy.wait()

    def drain(zs):
        for s in range(len(SETS)):
            if len(key_sites(zs, SETS[s])) > 1:
                for t in (K, V):
                    wait_slabs(back_recv.at[t, s, 0], 4)
            for t in range(4):
                wait_slabs(in_send.at[t, s], sent[zs, t, s])
            if zs in SETS[s]:
                wait_slabs(o_send.at[s], sent[zs, "o", s])
                for t in range(3):
                    wait_slabs(back_send.at[t, s], sent[zs, "qkv"[t], s])

    for_each_z(drain)


def local(queries, key_vectors, value_vectors, out_weight, grad_out):
    shape = queries.shape
    flat = lambda a: a.reshape(ROWS, WIDTH)
    any_, vmem = pl.BlockSpec(memory_space=pl.ANY), pl.BlockSpec(memory_space=pltpu.VMEM)
    dma = lambda *n: pltpu.SemaphoreType.DMA(n)
    n = len(SETS)
    big = jax.ShapeDtypeStruct((ROWS, WIDTH), BF16)
    scratch = [pltpu.VMEM((16, PART, LANES), BF16)] * (5 * n)
    scratch += [pltpu.VMEM((ROWS, WIDTH), BF16)] * 3 + [pltpu.VMEM((2, 3, ROWS, WIDTH), BF16), pltpu.VMEM((ROWS, WIDTH), BF16)]
    scratch += [pltpu.VMEM((4, 8, 6, WIDTH), BF16), pltpu.VMEM((128, WIDTH), F32), pltpu.VMEM((WIDTH, WIDTH), BF16)]
    scratch += [
        pltpu.VMEM((WIDTH, WIDTH), BF16),
        pltpu.VMEM((4, 2, 96, WIDTH), BF16),
        pltpu.VMEM((4, 192, WIDTH), BF16),
        pltpu.VMEM((4, 192, WIDTH), BF16),
        pltpu.VMEM((4, 48, WIDTH), BF16),
        pltpu.VMEM((4, 48, WIDTH), BF16),
        pltpu.VMEM((8, 6, WIDTH), BF16),
        pltpu.VMEM((8, 6, WIDTH), BF16),
    ]
    scratch += [dma(3), dma(4, n), dma(4, n), dma(n), dma(n), dma(3, n), dma(3, n, 3)]
    scratch += [dma(8), dma(8), dma(4), dma(4), dma(4, 2), dma(4, 2), dma(4, 2), dma(4, 2)]
    scratch += [dma(4, 2), dma(4, 2), dma(4), dma(4), dma(4), dma(4), dma(8), dma(8)]
    proj, dq, dk, dv, dw = pl.pallas_call(
        kernel,
        out_shape=[big] * 4 + [jax.ShapeDtypeStruct((6, WIDTH), F32)],
        in_specs=[any_] * 5,
        out_specs=[any_] * 4 + [vmem],
        scratch_shapes=scratch,
        compiler_params=pltpu.CompilerParams(
            collective_id=0, has_side_effects=True, vmem_limit_bytes=63 * 2**20
        ),
    )(flat(queries), flat(key_vectors), flat(value_vectors), out_weight, flat(grad_out))
    return tuple(a.reshape(shape) for a in (proj, dq, dk, dv)) + (dw,)


def solution(mesh):
    tokens, rows = P("fsdp", "frame", None, None), P(("fsdp", "frame"), None)
    return jax.shard_map(
        local,
        mesh=mesh,
        in_specs=(tokens, tokens, tokens, rows, tokens),
        out_specs=(tokens, tokens, tokens, tokens, rows),
        check_vma=False,
    )
```

time: 1590 us -> 163 us (0.10)
  blocking collectives: 688 us -> 0 us
  starting transfers between devices: 597 us -> 0 us
  Pallas kernels: 0 us -> 156 us
  waiting for transfers between devices: 132 us -> 0 us
  local copies, waits for them, and re-layouts: 125 us -> 6.47 us
  matrix products: 22.1 us -> 0 us
    unnamed x1 -> x0, blocking collectives: 641 us -> none
    unnamed x64 -> x0, starting transfers between devices: 553 us -> none
    pallas_call x0 -> x1, Pallas kernels: none -> 156 us  [local(): pl.pallas_call(kernel, out_shape=[big] * 4 + [jax.ShapeDtypeStruct((6, WI...]
    all_to_all x8 -> x0, waiting for transfers between devices: 115 us -> none  [the longest x1 43.4 us: local(): lax.all_to_all(key_vectors, 'frame', split_axis=2, concat_axis=1, tiled=T...]
    unnamed x115 -> x13, local copies, waits for them, and re-layouts: 110 us -> 6.47 us
    all_gather x1 -> x0, blocking collectives: 46.2 us -> none  [local(): block = lax.all_gather(out_weight, 'frame', axis=0, tiled=True)]
    all_to_all x8 -> x0, starting transfers between devices: 43.7 us -> none  [the longest x1 9.75 us: local(): lax.all_to_all(key_vectors, 'frame', split_axis=2, concat_axis=1, tiled=T...]
    dot_general x8 -> x0, matrix products: 19.6 us -> none  [the longest x1 5.15 us: local(): lax.dot_general(flat, grad_flat, (((0,), (0,)), ((), ())), preferred_elem...]
  transfers between devices with their start and end apart: 73 -> 0, of which waited for: 15 -> 0; matrix products, arithmetic and copies ran while one was open for 49% -> 0% of each run, Pallas kernels for 0% -> 0%
where the time goes in v1:
time: 163 us
  Pallas kernels  156 us (96%)
  local copies, waits for them, and re-layouts  6.47 us (4%)
    pallas_call x1, Pallas kernels, local(): pl.pallas_call(kernel, out_shape=[big] * 4 + [jax.ShapeDtypeStruct((6, WI...  156 us
    unnamed x13, local copies, waits for them, and re-layouts  6.47 us

profile of v1, /device:TPU:2, one launch (start us, length us, event | category | flops | bytes accessed | tf_op | source)
XLA Modules:
  0.0 163.0 jit_solution(13701457628109237786)
XLA Ops:
  0.6 155.9 %shard_map.92 = (bf16[256,1536]{1,0:T(8,128)(2,1)}, bf16[256,1536]{1,0:T(8,128)(2,1)}, bf16[256,1536]{1,0:T(8,128)(2,1)}, bf16[256,1536]{1,0:T(8,128)(2,1)}, f32[6,1536]{1,0:T(8,128)}) custom-call(bf16[256,1536]{1,0:T(8,128)(2,1)} %bitcast.20, bf16[256,1536]{1,0:T(8,128)(2,1)} %bitcast.21, bf16[256,1536]{1,0:T(8,128)(2,1)} %bitcast.22, ...), custom_call_target="tpu_custom_call" | custom-call | tf_op jit(solution)/shard_map/pallas_call | solution.py:456
  156.5 0.0 copy-start.2
  156.5 2.1 %copy.19 = bf16[2,1,128,1536]{3,2,1,0:T(8,128)(2,1)} copy(bf16[2,1,128,1536]{3,2,1,0:T(8,128)(2,1)} %bitcast.19) | data formatting | bytes 1572864
  158.7 0.0 copy-done.2
  158.7 0.0 copy-start.1
  158.7 0.9 copy.20
  159.6 0.5 copy-done.1
  160.1 0.0 copy-start
  160.1 0.9 copy.21
  161.0 0.5 copy-done
  161.5 0.0 copy-start.3
  161.5 0.9 copy.22
  162.4 0.0 copy-done.3
  162.4 0.6 copy.23
Async XLA Ops:
  156.5 2.1 %copy-start.2 = (bf16[256,1536]{1,0:T(8,128)(2,1)S(1)}, bf16[256,1536]{1,0:T(8,128)(2,1)}, u32[]{:S(2)}) copy-start(bf16[256,1536]{1,0:T(8,128)(2,1)} %get-tuple-element.11) | copy-start | bytes 2359300
  158.7 1.4 copy-start.1
  160.1 1.4 copy-start
  161.5 0.9 copy-start.3

commit v2 on v1

v2 whole, which is shorter than its diff:
```python
import functools

import jax
import jax.numpy as jnp
from jax import lax
from jax.experimental import pallas as pl
from jax.experimental.pallas import tpu as pltpu
from jax.sharding import PartitionSpec as P

MESH = pl.DeviceIdType.MESH
F32, BF16 = jnp.float32, jnp.bfloat16
HEAD = 128
ROWS = 256
PART = 64
BAND = 16
WIDTH = 1536
LANES = 512
FACTOR = HEAD ** -0.5
TOKEN_FACTOR = 65536.0 ** -0.5
SETS = ((1, 1, 1, 1), (0, 0, 2, 2), (0, 0, 3, 3))
Q, K, V, G = range(4)
NT = (((1,), (1,)), ((), ()))
TN = (((0,), (0,)), ((), ()))


def dot(a, b, dims=(((1,), (0,)), ((), ()))):
    return lax.dot_general(a, b, dims, preferred_element_type=F32)


def query_blocks(site, where):
    return [b for b in range(4) if where[b] == site]


def key_sites(block, where):
    return [s for s in sorted(set(where)) if block <= max(query_blocks(s, where))]


def lanes_of(s):
    return pl.ds(LANES * s, LANES)


def kernel(q_in, k_in, v_in, w_in, g_in, proj_out, dq_out, dk_out, dv_out, dw_out, *refs):
    refs = list(refs)
    take = lambda n: [refs.pop(0) for _ in range(n)]
    held = [take(4) for _ in SETS]
    attended = take(len(SETS))
    (partial,) = take(1)
    g_home, o_home, ga_home, proj_home = take(4)
    w_slabs, w_pad, w_full = take(3)
    x_own, x_out, x_in, y_out, y_in, z_out, z_in = take(7)
    local_sem, in_send, iy_recv, iz_recv, o_send, o_recv, by_send, home_recv = take(8)
    wz_send, wz_recv, wy_send, wy_recv, wx_send, wx_recv, wc_send, wc_recv = take(8)
    gc_send, gc_recv, oc_send, oc_recv, dx_send, dx_recv, dy_send, dy_recv, dz_send, dz_recv = take(10)

    f = lax.axis_index("fsdp")
    fr = lax.axis_index("frame")
    x, zh, core = f // 4, lax.rem(f // 2, 2), lax.rem(f, 2)
    z, y = fr // 4, lax.rem(fr, 4)
    z8 = zh * 4 + z

    def z_device(d):
        t = lax.rem(z8 + d, 8)
        return {"fsdp": x * 4 + (t // 4) * 2 + core, "frame": lax.rem(t, 4) * 4 + y}

    def y_device(d):
        return {"frame": z * 4 + lax.rem(y + d, 4)}

    def x_device(d):
        return {"fsdp": lax.rem(x + d, 4) * 4 + lax.rem(f, 4)}

    other_core = {"fsdp": f + 1 - 2 * core}

    def remote(src, dst, send, recv, device):
        return pltpu.make_async_remote_copy(
            src_ref=src, dst_ref=dst, send_sem=send, recv_sem=recv, device_id=device, device_id_type=MESH
        )

    def wait_slabs(sem, n):
        if n:
            ref = held[0][0].at[pl.ds(0, n)]
            pltpu.make_async_copy(ref, ref, sem).wait()

    barrier = pltpu.get_barrier_semaphore()
    partners = [{"frame": lax.rem(fr + d, 16)} for d in range(1, 16)]
    partners += [{"fsdp": x * 4 + (1 - zh) * 2 + core, "frame": k * 4 + y} for k in range(4)]
    partners += [x_device(d) for d in (1, 2, 3)] + [other_core]
    for device in partners:
        pl.semaphore_signal(barrier, inc=1, device_id=device, device_id_type=MESH)
    pl.semaphore_wait(barrier, len(partners))

    g_load = pltpu.make_async_copy(g_in, g_home.at[0], local_sem.at[0])
    g_load.start()
    own_rows = pltpu.make_async_copy(w_in, w_slabs.at[y, z8], local_sem.at[1])
    own_rows.start()
    wz = [
        remote(w_in, w_slabs.at[y, z8], wz_send.at[d], wz_recv.at[d], z_device(d)) for d in range(1, 8)
    ]
    for c in wz:
        c.start()

    def at(places, fn, *args):
        for zs in places:
            pl.when(z == zs)(functools.partial(fn, zs, *args))

    every = range(4)
    sent = {}

    def part(ref, j, s):
        return ref.at[pl.ds(pl.multiple_of(j * PART, PART), PART), lanes_of(s)]

    def own(ref, zs):
        return ref.at[pl.ds(4 * zs, 4)]

    def sites_for(b, t, s):
        return [SETS[s][b]] if t in (Q, G) else key_sites(b, SETS[s])

    def others(b, t, s):
        return sorted((a for a in sites_for(b, t, s) if a != b), key=lambda a: -abs(a - b))

    def send_in(zs, t, s):
        src = (q_in, k_in, v_in, ga_home)[t]
        count = 0
        for site in others(zs, t, s) + [zs]:
            if site not in sites_for(zs, t, s):
                continue
            recv = (iy_recv if site == zs else iz_recv).at[t, s]
            for d in (2, 1, 3, 0):
                j = lax.rem(y + d, 4)
                if site == zs and d == 0:
                    pltpu.make_async_copy(part(src, j, s), held[s][t].at[fr], recv).start()
                else:
                    device = {"frame": site * 4 + j}
                    remote(part(src, j, s), held[s][t].at[fr], in_send.at[t, s], recv, device).start()
                    count += 1
        sent["in", zs, t, s] = count

    def wait_in(zs, t, s):
        blocks = query_blocks(zs, SETS[s])
        wait_slabs(iy_recv.at[t, s], 4)
        wait_slabs(iz_recv.at[t, s], 4 * (len(blocks) - 1) if t in (Q, G) else 4 * max(blocks))

    def home(zs, s, b, src, dst, send_sem, recv_sem):
        for d in (2, 1, 3, 0):
            frame = 4 * b + lax.rem(y + d, 4)
            if b == zs and d == 0:
                pltpu.make_async_copy(src.at[frame], dst, recv_sem).start()
            else:
                remote(src.at[frame], dst, send_sem, recv_sem, {"frame": frame}).start()
        return 3 if b == zs else 4

    def geometry(zs, s):
        blocks = query_blocks(zs, SETS[s])
        return 4 * blocks[0], 4 * (blocks[-1] + 1), 4 * (blocks[-1] + 1)

    def bias_of(first, last, keys):
        shape = ((last - first) * BAND, keys * BAND)
        row = lax.broadcasted_iota(jnp.int32, shape, 0)
        col = lax.broadcasted_iota(jnp.int32, shape, 1)
        allowed = ((row & 15) == (col & 15)) & ((row >> 4) + first >= (col >> 4))
        return jnp.where(allowed, 0.0, -jnp.inf).astype(F32)

    def probs_of(queries, keys, bias):
        scores = [dot(a, b, NT) * FACTOR + bias for a, b in zip(queries, keys)]
        top = [jnp.max(a, axis=1, keepdims=True) for a in scores]
        e = [jnp.exp(a - b) for a, b in zip(scores, top)]
        scale = [1.0 / jnp.sum(a, axis=1, keepdims=True) for a in e]
        return [a * b for a, b in zip(e, scale)]

    def heads(fn):
        def step(h, carry):
            fn(pl.ds(pl.multiple_of(h * HEAD, HEAD), HEAD))
            return carry

        lax.fori_loop(0, 4, step, 0)

    bands = [pl.ds(p * BAND, BAND) for p in range(4)]

    def load(ref, a, b, lanes):
        return [ref[a:b, rows, lanes].reshape((b - a) * BAND, HEAD) for rows in bands]

    def store(ref, a, b, lanes, values):
        for rows, value in zip(bands, values):
            ref[a:b, rows, lanes] = value.astype(BF16).reshape(b - a, BAND, HEAD)

    def forward(zs, s):
        first, last, keys = geometry(zs, s)
        for t in (K, V, Q):
            wait_in(zs, t, s)
        bias = bias_of(first, last, keys)

        def head(lanes):
            queries, keys_ = load(held[s][Q], first, last, lanes), load(held[s][K], 0, keys, lanes)
            values = load(held[s][V], 0, keys, lanes)
            weights = [a.astype(BF16) for a in probs_of(queries, keys_, bias)]
            store(attended[s], first, last, lanes, [dot(a, b) for a, b in zip(weights, values)])

        heads(head)
        sent["o", zs, 0, s] = sum(
            home(zs, s, b, attended[s], part(o_home.at[0], y, s), o_send.at[s], o_recv.at[s])
            for b in sorted(query_blocks(zs, SETS[s]), key=lambda b: -abs(b - zs))
        )

    def backward(zs, s):
        first, last, keys = geometry(zs, s)
        wait_in(zs, G, s)
        bias = bias_of(first, last, keys)

        def head(lanes):
            queries, keys_ = load(held[s][Q], first, last, lanes), load(held[s][K], 0, keys, lanes)
            values, grads = load(held[s][V], 0, keys, lanes), load(held[s][G], first, last, lanes)
            grad_probs = [dot(a, b, NT) for a, b in zip(grads, values)]
            probs = probs_of(queries, keys_, bias)
            centre = [jnp.sum(a * b, axis=1, keepdims=True) for a, b in zip(probs, grad_probs)]
            grad_scores = [(a * (b - c)).astype(BF16) for a, b, c in zip(probs, grad_probs, centre)]
            weights = [a.astype(BF16) for a in probs]
            grad_q = [dot(a, b) * FACTOR for a, b in zip(grad_scores, keys_)]
            grad_k = [dot(a, b, TN) * FACTOR for a, b in zip(grad_scores, queries)]
            grad_v = [dot(a, b, TN) for a, b in zip(weights, grads)]
            store(held[s][Q], first, last, lanes, grad_q)
            store(held[s][K], 0, keys, lanes, grad_k)
            store(held[s][V], 0, keys, lanes, grad_v)

        heads(head)
        for t in (K, V, Q):
            blocks = query_blocks(zs, SETS[s]) if t == Q else range(keys // 4)
            count = 0
            for b in sorted(blocks, key=lambda b: -abs(b - zs)):
                sites = sites_for(b, t, s)
                slot = sites.index(zs)
                dst = (dq_out, dk_out, dv_out)[t]
                dst = part(dst, y, s) if len(sites) == 1 else part(partial.at[t - K, s, slot], y, 0)
                count += home(zs, s, b, held[s][t], dst, by_send.at[t, s], home_recv.at[t, s, slot])
            sent["back", zs, t, s] = count

    def arrived(zs, t, s):
        n = len(sites_for(zs, t, s))
        for slot in range(n):
            wait_slabs(home_recv.at[t, s, slot], 4)
        if n > 1:
            terms = partial.at[t - K, s]

            def add(i, carry):
                rows = pl.ds(pl.multiple_of(i * PART, PART), PART)
                total = terms[0, rows, :].astype(F32)
                for slot in range(1, n):
                    total += terms[slot, rows, :].astype(F32)
                terms[0, rows, :] = total.astype(BF16)
                return carry

            lax.fori_loop(0, ROWS // PART, add, 0)
            dst = (dq_out, dk_out, dv_out)[t]
            pltpu.make_async_copy(terms.at[0], dst.at[:, lanes_of(s)], home_recv.at[t, s, 0]).start()

    def stored(zs, t, s):
        if len(sites_for(zs, t, s)) > 1:
            wait_slabs(home_recv.at[t, s, 0], 4)

    def sites_of(s):
        return sorted(set(SETS[s]))

    g_other = remote(g_in, g_home.at[1], gc_send.at[0], gc_recv.at[0], other_core)
    g_other.start()
    for c in wz:
        c.wait()
    own_rows.wait()
    wy = [
        remote(w_slabs.at[y], w_slabs.at[y], wy_send.at[d], wy_recv.at[d], y_device(d)) for d in (1, 2, 3)
    ]
    for c in wy:
        c.start()

    for s in range(len(SETS)):
        for t in (K, V, Q):
            at(every, send_in, t, s)

    w_pad[...] = jnp.zeros_like(w_pad)
    r = lax.broadcasted_iota(jnp.int32, (96, 128), 0)
    c_ = lax.broadcasted_iota(jnp.int32, (96, 128), 1)
    sixth = (r * 171) >> 10
    pick = jnp.where(c_ == r + 2 * sixth, 1.0, 0.0).astype(BF16)
    for c in wy:
        c.wait()

    def w_rows(xx, h, cc):
        return w_full.at[pl.ds(pl.multiple_of((4 * xx + 2 * h + cc) * 96, 96), 96)]

    def x_from(d):
        return lax.rem(x + 4 - d, 4)

    def core_copy(d, h):
        ref = w_rows(x_from(d), h, core)
        return remote(ref, ref, wc_send.at[d, h], wc_recv.at[d, h], other_core)

    wx = {}
    for h in range(2):
        for i in range(16):
            w_pad[8 * i : 8 * i + 6, :] = w_slabs[i % 4, 4 * h + i // 4].astype(F32)
        w_rows(x, h, core)[...] = dot(pick, w_pad[...].astype(BF16)).astype(BF16)
        for d in (1, 3):
            wx[d, h] = remote(w_rows(x, h, core), w_rows(x, h, core), wx_send.at[d, h], wx_recv.at[d, h], x_device(d))
            wx[d, h].start()
        core_copy(0, h).start()
    for h in range(2):
        wx[2, h] = remote(w_rows(x, h, core), w_rows(x, h, core), wx_send.at[2, h], wx_recv.at[2, h], x_device(2))
        wx[2, h].start()

    at(sites_of(0), forward, 0)
    at(sites_of(1), forward, 1)

    def pass_on(d):
        for h in range(2):
            wx[d, h].wait()
            core_copy(d, h).start()

    pass_on(1)
    pass_on(3)
    at(sites_of(2), forward, 2)
    pass_on(2)

    for d in range(4):
        for h in range(2):
            core_copy(d, h).wait()
    g_load.wait()
    for s in range(len(SETS)):
        ga_home[:, lanes_of(s)] = dot(g_home[0], w_full[LANES * s : LANES * (s + 1), :], NT).astype(BF16)
        at(every, send_in, G, s)

    o_other = []
    for s in range(len(SETS)):
        wait_slabs(o_recv.at[s], 4)
        c = remote(
            o_home.at[0, :, lanes_of(s)], o_home.at[1, :, lanes_of(s)], oc_send.at[s], oc_recv.at[s], other_core
        )
        c.start()
        o_other.append(c)

    g_other.wait()
    for c in o_other:
        c.wait()
    r = lax.broadcasted_iota(jnp.int32, (384, 192), 0)
    c_ = lax.broadcasted_iota(jnp.int32, (384, 192), 1)
    side = jnp.where(r == c_ + 96 * core + jnp.where(c_ >= 96, 96, 0), 1.0, 0.0).astype(BF16)
    dx = {}
    for d in (2, 1, 3, 0):
        block = pl.ds(pl.multiple_of(lax.rem(x + d, 4) * 384, 384), 384)
        left = dot(o_home[:, :, block].reshape(2 * ROWS, 384), side).astype(BF16)
        for n in range(3):
            cols = pl.ds(n * LANES, LANES)
            term = dot(left, g_home[:, :, cols].reshape(2 * ROWS, LANES), TN) * TOKEN_FACTOR
            if d:
                x_out[d, :, cols] = term.astype(BF16)
            else:
                x_own[:, cols] = term
        if d:
            dx[d] = remote(x_out.at[d], x_in.at[d], dx_send.at[d], dx_recv.at[d], x_device(d))
            dx[d].start()

    for s in range(len(SETS)):
        at(sites_of(s), backward, s)

    for n in range(3):
        cols = pl.ds(n * LANES, LANES)
        proj_home[:, cols] = dot(o_home[0], w_full[:, cols]).astype(BF16)
    proj_copy = pltpu.make_async_copy(proj_home, proj_out, local_sem.at[2])
    proj_copy.start()

    for d in (1, 2, 3):
        dx[d].wait()
    r = lax.broadcasted_iota(jnp.int32, (192, 192), 0)
    c_ = lax.broadcasted_iota(jnp.int32, (192, 192), 1)
    slab = (r * 171) >> 10
    source = 24 * (slab & 7) + 6 * (slab >> 3) + (r - 6 * slab)
    order = jnp.where(c_ == source, 1.0, 0.0).astype(BF16)
    for n in range(3):
        cols = pl.ds(n * LANES, LANES)
        total = x_own[:, cols]
        for d in (1, 2, 3):
            total += x_in[d, :, cols].astype(F32)
        y_out[:, :, cols] = dot(order, total.astype(BF16)).astype(BF16).reshape(4, 48, LANES)
    dy = {}
    for d in (1, 2, 3):
        dy[d] = remote(y_out.at[lax.rem(y + d, 4)], y_in.at[d], dy_send.at[d], dy_recv.at[d], y_device(d))
        dy[d].start()

    for d in (1, 2, 3):
        dy[d].wait()
    r = lax.broadcasted_iota(jnp.int32, (64, 48), 0)
    c_ = lax.broadcasted_iota(jnp.int32, (64, 48), 1)
    apart = jnp.where((c_ == r - 2 * (r >> 3)) & ((r & 7) < 6), 1.0, 0.0).astype(BF16)
    total = y_out[y].astype(F32)
    for d in (1, 2, 3):
        total += y_in[d].astype(F32)
    slabs = dot(apart, total.astype(BF16))
    for i in range(8):
        z_out[i] = slabs[8 * i : 8 * i + 6].astype(BF16)
    dz = {}
    for d in range(1, 8):
        dz[d] = remote(z_out.at[lax.rem(z8 + d, 8)], z_in.at[d], dz_send.at[d], dz_recv.at[d], z_device(d))
        dz[d].start()

    for s in range(len(SETS)):
        for t in (K, V, Q):
            at(every, arrived, t, s)

    for d in range(1, 8):
        dz[d].wait()
    total = z_out[z8].astype(F32)
    for d in range(1, 8):
        total += z_in[d].astype(F32)
    dw_out[...] = total

    proj_copy.wait()

    def drain(zs):
        for s in range(len(SETS)):
            for t in range(4):
                wait_slabs(in_send.at[t, s], sent["in", zs, t, s])
            for t in (K, V, Q):
                stored(zs, t, s)
            if zs in SETS[s]:
                wait_slabs(o_send.at[s], sent["o", zs, 0, s])
                for t in (K, V, Q):
                    wait_slabs(by_send.at[t, s], sent["back", zs, t, s])

    at(every, drain)


def hand_on(*refs):
    n = len(refs) // 3
    sources, results, held, sem = refs[:n], refs[n : 2 * n], refs[2 * n : 3 * n], refs[3 * n]
    loads = [pltpu.make_async_copy(a, b, sem.at[i]) for i, (a, b) in enumerate(zip(sources, held))]
    stores = [pltpu.make_async_copy(a, b, sem.at[i]) for i, (a, b) in enumerate(zip(held, results))]
    for c in loads:
        c.start()
    for c, d in zip(loads, stores):
        c.wait()
        d.start()
    for c in stores:
        c.wait()


def local(queries, key_vectors, value_vectors, out_weight, grad_out):
    shape = queries.shape
    flat = lambda a: a.reshape(ROWS, WIDTH)
    any_, vmem = pl.BlockSpec(memory_space=pl.ANY), pl.BlockSpec(memory_space=pltpu.VMEM)
    dma = lambda *n: pltpu.SemaphoreType.DMA(n)
    n = len(SETS)
    big = jax.ShapeDtypeStruct((ROWS, WIDTH), BF16)
    scratch = [pltpu.VMEM((16, PART, LANES), BF16)] * (5 * n)
    scratch += [pltpu.VMEM((2, n, 2, ROWS, LANES), BF16)]
    scratch += [pltpu.VMEM((2, ROWS, WIDTH), BF16)] * 2 + [pltpu.VMEM((ROWS, WIDTH), BF16)] * 2
    scratch += [pltpu.VMEM((4, 8, 6, WIDTH), BF16), pltpu.VMEM((128, WIDTH), F32), pltpu.VMEM((WIDTH, WIDTH), BF16)]
    scratch += [
        pltpu.VMEM((192, WIDTH), F32),
        pltpu.VMEM((4, 192, WIDTH), BF16),
        pltpu.VMEM((4, 192, WIDTH), BF16),
        pltpu.VMEM((4, 48, WIDTH), BF16),
        pltpu.VMEM((4, 48, WIDTH), BF16),
        pltpu.VMEM((8, 6, WIDTH), BF16),
        pltpu.VMEM((8, 6, WIDTH), BF16),
    ]
    scratch += [dma(3), dma(4, n), dma(4, n), dma(4, n)]
    scratch += [dma(n), dma(n), dma(3, n), dma(3, n, 2)]
    scratch += [dma(8), dma(8), dma(4), dma(4), dma(4, 2), dma(4, 2), dma(4, 2), dma(4, 2)]
    scratch += [dma(1), dma(1), dma(n), dma(n), dma(4), dma(4), dma(4), dma(4), dma(8), dma(8)]
    proj, dq, dk, dv, dw = pl.pallas_call(
        kernel,
        out_shape=[big] * 4 + [jax.ShapeDtypeStruct((6, WIDTH), F32)],
        in_specs=[any_] * 5,
        out_specs=[any_] * 4 + [vmem],
        scratch_shapes=scratch,
        compiler_params=pltpu.CompilerParams(
            collective_id=0, has_side_effects=True, vmem_limit_bytes=63 * 2**20
        ),
    )(flat(queries), flat(key_vectors), flat(value_vectors), out_weight, flat(grad_out))
    results = (proj, dq, dk, dv, dw)
    proj, dq, dk, dv, dw = pl.pallas_call(
        hand_on,
        out_shape=[jax.ShapeDtypeStruct(a.shape, a.dtype) for a in results],
        in_specs=[any_] * 5,
        out_specs=[any_] * 5,
        scratch_shapes=[pltpu.VMEM(a.shape, a.dtype) for a in results] + [dma(5)],
    )(*results)
    return tuple(a.reshape(shape) for a in (proj, dq, dk, dv)) + (dw,)


def solution(mesh):
    tokens, rows = P("fsdp", "frame", None, None), P(("fsdp", "frame"), None)
    return jax.shard_map(
        local,
        mesh=mesh,
        in_specs=(tokens, tokens, tokens, rows, tokens),
        out_specs=(tokens, tokens, tokens, tokens, rows),
        check_vma=False,
    )
```

time: 163 us -> 151 us (0.926)
  Pallas kernels: 156 us -> 149 us
  local copies, waits for them, and re-layouts: 6.47 us -> 0 us
    pallas_call x1, Pallas kernels: 156 us -> 146 us  [local(): pl.pallas_call(kernel, out_shape=[big] * 4 + [jax.ShapeDtypeStruct((6, WI...]
    unnamed x13 -> x0, local copies, waits for them, and re-layouts: 6.47 us -> none
    pallas_call x0 -> x1, Pallas kernels: none -> 2.83 us  [local(): pl.pallas_call(hand_on, out_shape=[jax.ShapeDtypeStruct(a.shape, a.dtype)...]
where the time goes in v2:
time: 151 us; the launch traced here: 150 us
  Pallas kernels  149 us (99%)
    pallas_call x1, Pallas kernels, local(): pl.pallas_call(kernel, out_shape=[big] * 4 + [jax.ShapeDtypeStruct((6, WI...  146 us

profile of v2, /device:TPU:2, one launch (start us, length us, event | category | flops | bytes accessed | tf_op | source)
XLA Modules:
  0.0 150.1 jit_solution(4981915870709708681)
XLA Ops:
  0.6 146.4 %shard_map.92 = (bf16[256,1536]{1,0:T(8,128)(2,1)}, bf16[256,1536]{1,0:T(8,128)(2,1)}, bf16[256,1536]{1,0:T(8,128)(2,1)}, bf16[256,1536]{1,0:T(8,128)(2,1)}, f32[6,1536]{1,0:T(8,128)}) custom-call(bf16[256,1536]{1,0:T(8,128)(2,1)} %bitcast.16, bf16[256,1536]{1,0:T(8,128)(2,1)} %bitcast.17, bf16[256,1536]{1,0:T(8,128)(2,1)} %bitcast.18, ...), custom_call_target="tpu_custom_call" | custom-call | tf_op jit(solution)/shard_map/pallas_call | solution.py:466
  147.1 2.8 %shard_map.93 = (bf16[256,1536]{1,0:T(8,128)(2,1)}, bf16[256,1536]{1,0:T(8,128)(2,1)}, bf16[256,1536]{1,0:T(8,128)(2,1)}, bf16[256,1536]{1,0:T(8,128)(2,1)}, f32[6,1536]{1,0:T(8,128)}) custom-call(bf16[256,1536]{1,0:T(8,128)(2,1)} %get-tuple-element.15.refs_0_, bf16[256,1536]{1,0:T(8,128)(2,1)} %get-tuple-element.16.refs_1_, ...), custom_call_target="tpu_custom_call" | custom-call | tf_op jit(solution)/shard_map/pallas_call | solution.py:477

commit v3 on v2

--- a/solution.py
+++ b/solution.py
@@ -221,16 +221,19 @@
             store(held[s][V], 0, keys, lanes, grad_v)
 
         heads(head)
-        for t in (K, V, Q):
-            blocks = query_blocks(zs, SETS[s]) if t == Q else range(keys // 4)
-            count = 0
-            for b in sorted(blocks, key=lambda b: -abs(b - zs)):
-                sites = sites_for(b, t, s)
-                slot = sites.index(zs)
-                dst = (dq_out, dk_out, dv_out)[t]
-                dst = part(dst, y, s) if len(sites) == 1 else part(partial.at[t - K, s, slot], y, 0)
-                count += home(zs, s, b, held[s][t], dst, by_send.at[t, s], home_recv.at[t, s, slot])
-            sent["back", zs, t, s] = count
+        for t in (K, V):
+            give_back(zs, t, s)
+
+    def give_back(zs, t, s):
+        blocks = query_blocks(zs, SETS[s]) if t == Q else range(geometry(zs, s)[2] // 4)
+        count = 0
+        for b in sorted(blocks, key=lambda b: -abs(b - zs)):
+            sites = sites_for(b, t, s)
+            slot = sites.index(zs)
+            dst = (dq_out, dk_out, dv_out)[t]
+            dst = part(dst, y, s) if len(sites) == 1 else part(partial.at[t - K, s, slot], y, 0)
+            count += home(zs, s, b, held[s][t], dst, by_send.at[t, s], home_recv.at[t, s, slot])
+        sent["back", zs, t, s] = count
 
     def arrived(zs, t, s):
         n = len(sites_for(zs, t, s))
@@ -296,34 +299,47 @@
         for i in range(16):
             w_pad[8 * i : 8 * i + 6, :] = w_slabs[i % 4, 4 * h + i // 4].astype(F32)
         w_rows(x, h, core)[...] = dot(pick, w_pad[...].astype(BF16)).astype(BF16)
-        for d in (1, 3):
-            wx[d, h] = remote(w_rows(x, h, core), w_rows(x, h, core), wx_send.at[d, h], wx_recv.at[d, h], x_device(d))
-            wx[d, h].start()
+        for step in (1, 3) if h == 0 else (3, 1):
+            ref = w_rows(x, h, core)
+            wx[step, h] = remote(ref, ref, wx_send.at[step, h], wx_recv.at[step, h], x_device(step))
+            wx[step, h].start()
         core_copy(0, h).start()
-    for h in range(2):
-        wx[2, h] = remote(w_rows(x, h, core), w_rows(x, h, core), wx_send.at[2, h], wx_recv.at[2, h], x_device(2))
-        wx[2, h].start()
+
+    def pass_on(d, h, step=0):
+        wx[d, h].wait()
+        if step:
+            ref = w_rows(x_from(d), h, core)
+            wx[2, h] = remote(ref, ref, wx_send.at[2, h], wx_recv.at[2, h], x_device(step))
+            wx[2, h].start()
+        core_copy(d, h).start()
+
+    pass_on(1, 0, 1)
+    pass_on(3, 1, 3)
 
     at(sites_of(0), forward, 0)
     at(sites_of(1), forward, 1)
-
-    def pass_on(d):
-        for h in range(2):
-            wx[d, h].wait()
-            core_copy(d, h).start()
-
-    pass_on(1)
-    pass_on(3)
+    pass_on(1, 1)
+    pass_on(3, 0)
+
     at(sites_of(2), forward, 2)
-    pass_on(2)
-
-    for d in range(4):
+    pass_on(2, 0)
+    pass_on(2, 1)
+
+    def grad_attended(s):
+        ga_home[:, lanes_of(s)] = dot(g_home[0], w_full[LANES * s : LANES * (s + 1), :], NT).astype(BF16)
+        at(every, send_in, G, s)
+
+    g_load.wait()
+    for d in (0, 1, 3):
         for h in range(2):
             core_copy(d, h).wait()
-    g_load.wait()
-    for s in range(len(SETS)):
-        ga_home[:, lanes_of(s)] = dot(g_home[0], w_full[LANES * s : LANES * (s + 1), :], NT).astype(BF16)
-        at(every, send_in, G, s)
+    for side, s in ((x < 2, 0), (x >= 2, 2)):
+        pl.when(side)(functools.partial(grad_attended, s))
+    for h in range(2):
+        core_copy(2, h).wait()
+    grad_attended(1)
+    for side, s in ((x < 2, 2), (x >= 2, 0)):
+        pl.when(side)(functools.partial(grad_attended, s))
 
     o_other = []
     for s in range(len(SETS)):
@@ -398,6 +414,8 @@
         dz[d] = remote(z_out.at[lax.rem(z8 + d, 8)], z_in.at[d], dz_send.at[d], dz_recv.at[d], z_device(d))
         dz[d].start()
 
+    for s in range(len(SETS)):
+        at(sites_of(s), give_back, Q, s)
     for s in range(len(SETS)):
         for t in (K, V, Q):
             at(every, arrived, t, s)

time: 151 us -> 145 us (0.960)
  Pallas kernels: 149 us -> 143 us
    pallas_call x1, Pallas kernels: 146 us -> 140 us  [local(): pl.pallas_call(kernel, out_shape=[big] * 4 + [jax.ShapeDtypeStruct((6, WI...]
where the time goes in v3:
time: 145 us; the launch traced here: 143 us
  Pallas kernels  143 us (99%)
    pallas_call x1, Pallas kernels, local(): pl.pallas_call(kernel, out_shape=[big] * 4 + [jax.ShapeDtypeStruct((6, WI...  140 us

profile of v3, /device:TPU:2, one launch (start us, length us, event | category | flops | bytes accessed | tf_op | source)
XLA Modules:
  0.0 143.4 jit_solution(16669142227632782190)
XLA Ops:
  0.6 139.7 %shard_map.92 = (bf16[256,1536]{1,0:T(8,128)(2,1)}, bf16[256,1536]{1,0:T(8,128)(2,1)}, bf16[256,1536]{1,0:T(8,128)(2,1)}, bf16[256,1536]{1,0:T(8,128)(2,1)}, f32[6,1536]{1,0:T(8,128)}) custom-call(bf16[256,1536]{1,0:T(8,128)(2,1)} %bitcast.16, bf16[256,1536]{1,0:T(8,128)(2,1)} %bitcast.17, bf16[256,1536]{1,0:T(8,128)(2,1)} %bitcast.18, ...), custom_call_target="tpu_custom_call" | custom-call | tf_op jit(solution)/shard_map/pallas_call | solution.py:484
  140.4 2.8 %shard_map.93 = (bf16[256,1536]{1,0:T(8,128)(2,1)}, bf16[256,1536]{1,0:T(8,128)(2,1)}, bf16[256,1536]{1,0:T(8,128)(2,1)}, bf16[256,1536]{1,0:T(8,128)(2,1)}, f32[6,1536]{1,0:T(8,128)}) custom-call(bf16[256,1536]{1,0:T(8,128)(2,1)} %get-tuple-element.15.refs_0_, bf16[256,1536]{1,0:T(8,128)(2,1)} %get-tuple-element.16.refs_1_, ...), custom_call_target="tpu_custom_call" | custom-call | tf_op jit(solution)/shard_map/pallas_call | solution.py:495

commit v4 on v3

--- a/solution.py
+++ b/solution.py
@@ -374,12 +374,6 @@
     for s in range(len(SETS)):
         at(sites_of(s), backward, s)
 
-    for n in range(3):
-        cols = pl.ds(n * LANES, LANES)
-        proj_home[:, cols] = dot(o_home[0], w_full[:, cols]).astype(BF16)
-    proj_copy = pltpu.make_async_copy(proj_home, proj_out, local_sem.at[2])
-    proj_copy.start()
-
     for d in (1, 2, 3):
         dx[d].wait()
     r = lax.broadcasted_iota(jnp.int32, (192, 192), 0)
@@ -397,6 +391,12 @@
     for d in (1, 2, 3):
         dy[d] = remote(y_out.at[lax.rem(y + d, 4)], y_in.at[d], dy_send.at[d], dy_recv.at[d], y_device(d))
         dy[d].start()
+
+    for n in range(3):
+        cols = pl.ds(n * LANES, LANES)
+        proj_home[:, cols] = dot(o_home[0], w_full[:, cols]).astype(BF16)
+    proj_copy = pltpu.make_async_copy(proj_home, proj_out, local_sem.at[2])
+    proj_copy.start()
 
     for d in (1, 2, 3):
         dy[d].wait()

time: 145 us -> 145 us (level)
  no operation moved by 1% of the time
where the time goes in v4:
time: 145 us; the launch traced here: 143 us
  Pallas kernels  143 us (99%)
    pallas_call x1, Pallas kernels, local(): pl.pallas_call(kernel, out_shape=[big] * 4 + [jax.ShapeDtypeStruct((6, WI...  140 us

profile of v4, /device:TPU:2, one launch (start us, length us, event | category | flops | bytes accessed | tf_op | source)
XLA Modules:
  0.0 143.3 jit_solution(9603665718853434339)
XLA Ops:
  0.6 139.7 %shard_map.92 = (bf16[256,1536]{1,0:T(8,128)(2,1)}, bf16[256,1536]{1,0:T(8,128)(2,1)}, bf16[256,1536]{1,0:T(8,128)(2,1)}, bf16[256,1536]{1,0:T(8,128)(2,1)}, f32[6,1536]{1,0:T(8,128)}) custom-call(bf16[256,1536]{1,0:T(8,128)(2,1)} %bitcast.16, bf16[256,1536]{1,0:T(8,128)(2,1)} %bitcast.17, bf16[256,1536]{1,0:T(8,128)(2,1)} %bitcast.18, ...), custom_call_target="tpu_custom_call" | custom-call | tf_op jit(solution)/shard_map/pallas_call | solution.py:484
  140.3 2.8 %shard_map.93 = (bf16[256,1536]{1,0:T(8,128)(2,1)}, bf16[256,1536]{1,0:T(8,128)(2,1)}, bf16[256,1536]{1,0:T(8,128)(2,1)}, bf16[256,1536]{1,0:T(8,128)(2,1)}, f32[6,1536]{1,0:T(8,128)}) custom-call(bf16[256,1536]{1,0:T(8,128)(2,1)} %get-tuple-element.15.refs_0_, bf16[256,1536]{1,0:T(8,128)(2,1)} %get-tuple-element.16.refs_1_, ...), custom_call_target="tpu_custom_call" | custom-call | tf_op jit(solution)/shard_map/pallas_call | solution.py:495
